TPU v7x, 256 devices: a whole 4x4x8 slice. The times are simulated.
256 devices in a mesh: dp: 8 (over y, x_hi), tensor: 32 (over z, x_lo, core).
Axes of the slice: x: 4 (x_hi: 2, x_lo: 2; x = x_hi * 2 + x_lo), y: 4, z: 8, core: 2. Of those that a mesh axis runs over, the one named last changes fastest.
Arguments:
- hidden_in: bfloat16 [4096, 14848], P(('dp', 'tensor')), may hold values from -6 to 6
- norm_gain: bfloat16 [14848], replicated, may hold values from 0.5 to 1.5
- query_weight: bfloat16 [14848, 8192], P('dp', 'tensor'), may hold values from -0.046875 to 0.046875
- probe: bfloat16 [14848, 8192], P('dp', 'tensor'), may hold values from -0.046875 to 0.046875
- key_values: bfloat16 [4096, 1024], P(('dp', 'tensor')), may hold values from -6 to 6
- readout: bfloat16 [4096, 8192], P('dp', 'tensor'), may hold values from -0.0625 to 0.0625
- lengths: int32 [16, 2], P('dp'), may hold values from 32 to 128
- ref_margin: float32 [16], P('dp'), may hold values from -6 to 6
Outputs:
- hvp: float32 [14848, 8192], P('dp', 'tensor')
All inputs are finite; a program needn't handle non-finite values.
Results may differ from a plain program's by a relative error of at most 0.04.
Values may be sent and summed in bfloat16 or wider, within the bound.
No kernel may reach another device: no remote copies, remote signals or barrier semaphores. Data moves between devices by JAX's collectives and lax.ppermute only.
A program may use at most 128 MiB of HBM per device.

v0:
```python
import functools

import jax
import jax.numpy as jnp
from jax import lax
from jax.experimental import pallas as pl
from jax.experimental.pallas import tpu as pltpu
from jax.sharding import Mesh
from jax.sharding import PartitionSpec as P

HD = 64
KVH = 8
NY, NX, NZ, NL, NC = 4, 2, 8, 2, 2
DP = NY * NX
EARLY = 3

pair_beta = 0.5
norm_epsilon = 1e-05

bf16 = jnp.bfloat16
f32 = jnp.float32
CHUNKS = (0, 1, -1, 2, -2, 3, -3, 4)
LANES = 128


def toward(axis, size, shift):
    pairs = [((i + shift) % size, i) for i in range(size)]
    return lambda value: lax.ppermute(value, axis, pairs)


core_swap = toward("core", NC, 1)
lo_swap = toward("x_lo", NL, 1)
hi_swap = toward("x_hi", NX, 1)


def together(*values):
    return lax.optimization_barrier(values)


def dot(a, b):
    return jnp.dot(a, b, preferred_element_type=f32)


def reduce_y(partial, iy):
    split = partial.reshape(NY, NX, *partial.shape[1:])
    block = lambda dy: lax.dynamic_index_in_dim(split, lax.rem(iy + dy, NY), 0, False)
    total = block(0).astype(f32)
    for part in [toward("y", NY, -dy)(block(dy)) for dy in (2, 1, 3)]:
        total = total + part.astype(f32)
    return total


def hi_halves(total, ix):
    keep = lax.dynamic_index_in_dim(total, ix, 0, False)
    give = lax.dynamic_index_in_dim(total, 1 - ix, 0, False)
    return keep.astype(f32), hi_swap(give.astype(bf16))


def attention_kernel(info_ref, both_ref, read_ref, kv_ref, grad_ref, tan_ref, sums_ref, keys_ref, values_ref):
    places, sides, part_rows, columns = read_ref.shape
    seqs = kv_ref.shape[0]
    rows = sides * part_rows
    chunks = both_ref.shape[0] // rows
    pairs = columns // LANES
    per_seq = places // seqs
    scale = f32(HD**-0.5)
    nt = (((1,), (1,)), ((), ()))
    low = lax.broadcasted_iota(jnp.int32, (kv_ref.shape[1], LANES), 1) < HD
    for s in range(seqs):
        kv = kv_ref[s]
        turned = pltpu.roll(kv, HD, 1)
        keys_ref[s] = jnp.concatenate([jnp.where(low, kv, 0.0), jnp.where(low, 0.0, turned)]).astype(bf16)
        values_ref[s] = jnp.concatenate([jnp.where(low, turned, 0.0), jnp.where(low, 0.0, kv)]).astype(bf16)
    lane = lax.broadcasted_iota(jnp.int32, (part_rows, LANES), 1)
    row = lax.broadcasted_iota(jnp.int32, (part_rows, LANES), 0)
    out_lane = lax.broadcasted_iota(jnp.int32, (1, LANES), 1)
    x_lo, core = info_ref[chunks + seqs], info_ref[chunks + seqs + 1]
    stack = lambda blocks: jnp.concatenate(blocks, axis=0)
    column = lambda pair: slice(pair * LANES, (pair + 1) * LANES)
    sums = jnp.zeros((1, LANES), f32)
    for k in range(chunks):
        here = pl.ds(k * rows, rows)
        place = info_ref[k]
        seq = place // per_seq
        length = info_ref[chunks + seq]
        keys, values = keys_ref[seq], values_ref[seq]
        allowed, read = [], []
        for side in (x_lo, 1 - x_lo):
            position = ((place % per_seq * sides + side) * NC + core) * part_rows + row
            allowed.append(lane <= jnp.minimum(position, length - 1))
            live = position[:, :1] < length
            read.append(jnp.where(live, read_ref[place, side], 0.0))
        read = stack(read).astype(bf16)
        allowed = stack(allowed * pairs)
        both = both_ref[here, :].astype(bf16)
        both = lax.dot_general(
            stack([both[:, column(p)] for p in range(2 * pairs)]), keys, nt, preferred_element_type=f32
        )
        gain2 = lax.dot_general(
            stack([read[:, column(p)] for p in range(pairs)]), values, nt, preferred_element_type=f32
        )
        scores2, slope2 = both[: pairs * rows] * scale, both[pairs * rows :] * scale
        first, second = [], []
        logp = jnp.zeros((pairs * rows, 1), f32)
        logp_tan = jnp.zeros((pairs * rows, 1), f32)
        for head in range(2):
            part = column(head)
            scores = jnp.where(allowed, scores2[:, part], f32(-1e30))
            slope, gain = slope2[:, part], gain2[:, part]
            weights = jnp.exp(scores - jnp.max(scores, axis=1, keepdims=True))
            probs = weights / jnp.sum(weights, axis=1, keepdims=True)
            mean_gain = jnp.sum(probs * gain, axis=1, keepdims=True)
            mean_slope = jnp.sum(probs * slope, axis=1, keepdims=True)
            lean = gain - mean_gain
            pull = probs * (slope - mean_slope)
            mean_tan = jnp.sum(pull * lean, axis=1, keepdims=True)
            first.append((probs * lean).astype(bf16))
            second.append((pull * lean - probs * mean_tan).astype(bf16))
            logp = logp + mean_gain
            logp_tan = logp_tan + mean_tan
        out = dot(stack([jnp.concatenate(first, axis=1), jnp.concatenate(second, axis=1)]), keys) * scale
        for p in range(pairs):
            grad_ref[here, column(p)] = out[p * rows : (p + 1) * rows]
            tan_ref[here, column(p)] = out[(pairs + p) * rows : (pairs + p + 1) * rows]
        sums = sums + jnp.where(out_lane == seq, jnp.sum(logp), f32(0))
        sums = sums + jnp.where(out_lane == seq + LANES // 2, jnp.sum(logp_tan), f32(0))
    sums_ref[...] = sums


def attention(info, both, read, kv):
    rows, columns = both.shape[0], read.shape[-1]
    vmem = pl.BlockSpec(memory_space=pltpu.VMEM)
    return pl.pallas_call(
        attention_kernel,
        out_shape=(
            jax.ShapeDtypeStruct((rows, columns), f32),
            jax.ShapeDtypeStruct((rows, columns), f32),
            jax.ShapeDtypeStruct((1, LANES), f32),
        ),
        in_specs=[pl.BlockSpec(memory_space=pltpu.SMEM)] + [vmem] * 3,
        out_specs=(vmem, vmem, vmem),
        scratch_shapes=[pltpu.VMEM((kv.shape[0], 2 * kv.shape[1], LANES), bf16)] * 2,
        compiler_params=pltpu.CompilerParams(vmem_limit_bytes=24 * 1024 * 1024),
    )(info, both, read, kv)


def combine_kernel(chunks, seqs, info_ref, margin_ref, spread_ref, grad_ref, tan_ref, out_ref):
    total = jnp.sum(spread_ref[...], axis=0, keepdims=True)
    lane = lax.broadcasted_iota(jnp.int32, (1, LANES), 1)
    at = lambda i: jnp.sum(jnp.where(lane == i, total, f32(0)), axis=1, keepdims=True)
    coeffs = []
    for p in range(seqs // 2):
        margin = pair_beta * (at(2 * p) - at(2 * p + 1) - margin_ref[p])
        margin_tan = pair_beta * (at(LANES // 2 + 2 * p) - at(LANES // 2 + 2 * p + 1))
        sure, unsure = jax.nn.sigmoid(margin), jax.nn.sigmoid(-margin)
        slope = -pair_beta * unsure
        bend = pair_beta * unsure * sure * margin_tan
        coeffs += [(slope, bend), (-slope, -bend)]
    rows = grad_ref.shape[0] // chunks
    per_seq = NZ // seqs
    for k in range(chunks):
        seq = info_ref[k] // per_seq
        coeff, coeff_tan = coeffs[0]
        for s in range(1, seqs):
            coeff = jnp.where(seq == s, coeffs[s][0], coeff)
            coeff_tan = jnp.where(seq == s, coeffs[s][1], coeff_tan)
        here = pl.ds(k * rows, rows)
        out_ref[here, :] = coeff_tan * grad_ref[here, :] + coeff * tan_ref[here, :]


def combine(info, ref_margin, spread, grad, tan, seqs):
    vmem, smem = pl.BlockSpec(memory_space=pltpu.VMEM), pl.BlockSpec(memory_space=pltpu.SMEM)
    return pl.pallas_call(
        functools.partial(combine_kernel, len(CHUNKS), seqs),
        out_shape=jax.ShapeDtypeStruct(grad.shape, f32),
        in_specs=[smem, smem, vmem, vmem, vmem],
        out_specs=vmem,
    )(info, ref_margin, spread, grad, tan)


def shards(hidden_in, norm_gain, query_weight, probe, key_values, readout, lengths, ref_margin):
    iy, ix, iz, il, ic = (lax.axis_index(a) for a in ("y", "x_hi", "z", "x_lo", "core"))
    tensor = ("z", "x_lo", "core")
    rows_here, width = hidden_in.shape
    feats, columns = query_weight.shape

    wide = hidden_in.astype(f32)
    stats = jnp.mean(wide * wide, axis=1, keepdims=True)
    normed = (wide * lax.rsqrt(stats + norm_epsilon) * norm_gain.astype(f32)).astype(bf16)

    own = lax.all_to_all(normed, ("y", "x_hi"), split_axis=1, concat_axis=0, tiled=True)
    own = own.reshape(DP, rows_here, feats)
    other_q, other_t = core_swap(query_weight), core_swap(probe)
    own, other_q, other_t = together(own, other_q, other_t)
    message = {0: jnp.concatenate([own, lo_swap(own[:EARLY])])}
    (message[0],) = together(message[0])

    seqs = lengths.shape[0] * 2
    seq_len = NZ // seqs * NL * NC * rows_here

    def prepare(token):
        heads_kv, read, first, second, third, fourth, length, _ = together(
            key_values, readout, query_weight, other_q, probe, other_t, lengths, token
        )
        weights = jnp.concatenate([first, second, third, fourth], axis=1)
        heads_kv = heads_kv.reshape(rows_here, KVH, 2 * HD).swapaxes(0, 1)
        heads_kv = jnp.broadcast_to(heads_kv[:, None], (KVH, NL * NC, rows_here, 2 * HD))
        kv = lax.all_to_all(
            heads_kv.reshape(NZ * NL * NC, rows_here, 2 * HD), tensor, split_axis=0, concat_axis=0, tiled=True
        )
        kv = kv.reshape(seqs, seq_len, 2 * HD).astype(f32)
        read = read.reshape(NZ, NL, NC, rows_here, columns)
        mine = lax.dynamic_index_in_dim(read, ic, 2, False)
        theirs = lax.dynamic_index_in_dim(read, 1 - ic, 2, False)
        read = jnp.concatenate([mine, core_swap(theirs)], axis=-1).astype(f32)
        info = jnp.concatenate(
            [(iz + jnp.array(CHUNKS, jnp.int32) + NZ) % NZ, length.reshape(seqs), jnp.stack([il, ic])]
        )
        return weights, info, read, kv

    up, down = toward("z", NZ, -1), toward("z", NZ, 1)

    def rows_of(k):
        return jnp.stack([message[k][:DP], jnp.concatenate([message[k][DP:], late[k]])], axis=1)

    def multiply(group):
        block = jnp.stack([rows_of(k) for k in group], axis=1).reshape(DP, -1, feats)
        part = dot(block.reshape(-1, feats), weights).astype(bf16)
        return block, part.reshape(DP, block.shape[1], 4 * columns)

    def swap_late(k):
        both = lo_swap(jnp.stack([message[k][EARLY:DP], message[-k][EARLY:DP]]))
        return both[0], both[1]

    late = {}
    message[1], message[-1] = down(message[0]), up(message[0])
    late[0] = lo_swap(own[EARLY:])
    prepared = prepare(message[0])
    message[1], message[-1], late[0], *prepared = together(message[1], message[-1], late[0], *prepared)
    weights, info, read, kv = prepared
    message[2], message[-2] = down(message[1]), up(message[-1])
    late[1], late[-1] = swap_late(1)
    message[2], message[-2], late[1], late[-1] = together(message[2], message[-2], late[1], late[-1])
    message[3], message[-3] = down(message[2]), up(message[-2])
    late[2], late[-2] = swap_late(2)
    block_a, part_a = multiply((0, 1, -1))
    total_a = lax.psum_scatter(part_a.reshape(NY, -1, 4 * columns), "y", scatter_dimension=0, tiled=True)
    message[3], message[-3], late[2], late[-2], block_a = together(
        message[3], message[-3], late[2], late[-2], block_a
    )
    half = message[0].shape[0] // 2
    ends = down(message[3][:half]), up(message[-3][half:])
    late[3], late[-3] = swap_late(3)
    block_b, part_b = multiply((2, -2))
    total_b = reduce_y(part_b, iy)
    *ends, late[3], late[-3], block_b = together(*ends, late[3], late[-3], block_b)
    message[4] = jnp.concatenate(ends)
    late[4] = lo_swap(message[4][EARLY:DP])
    total_a = total_a.reshape(NX, -1, 4 * columns)
    keep_a, cross_a = hi_halves(total_a, ix)
    late[4], keep_a, total_b = together(late[4], keep_a, total_b)
    block_c, part_c = multiply((3, -3, 4))
    keep_b, cross_b = hi_halves(total_b, ix)
    arrived = lax.all_to_all(part_c, ("y", "x_hi"), split_axis=0, concat_axis=0, tiled=True)
    total_c = jnp.sum(arrived.astype(f32), axis=0)
    projected = jnp.concatenate([keep_a + cross_a.astype(f32), keep_b + cross_b.astype(f32), total_c])
    normed_all = jnp.concatenate([block_a, block_b, block_c], axis=1)

    grad, tan, sums = attention(info, projected, read, kv)
    spread = jnp.broadcast_to(sums[None], (NZ * NL * NC, 1, LANES))
    spread = lax.all_to_all(spread, tensor, split_axis=0, concat_axis=0, tiled=True).reshape(-1, LANES)
    hess_rows = combine(info, ref_margin, spread, grad, tan, seqs).astype(bf16)

    hess_all = jnp.broadcast_to(hess_rows[None], (DP, *hess_rows.shape))
    hess_all = lax.all_to_all(hess_all, ("y", "x_hi"), split_axis=0, concat_axis=0, tiled=True)
    hess_all = hess_all.reshape(-1, 2 * columns)
    left = normed_all.reshape(-1, feats)
    outer = lambda b: lax.dot_general(left, b, (((0,), (0,)), ((), ())), preferred_element_type=f32)
    theirs = core_swap(outer(hess_all[:, columns:]).astype(bf16))
    return outer(hess_all[:, :columns]) + theirs.astype(f32)


def solution(mesh):
    fine = Mesh(
        mesh.devices.reshape(NY, NX, NZ, NL, NC), ("y", "x_hi", "z", "x_lo", "core")
    )
    dp, tensor = ("y", "x_hi"), ("z", "x_lo", "core")
    return jax.shard_map(
        shards,
        mesh=fine,
        in_specs=(
            P(dp + tensor, None),
            P(),
            P(dp, tensor),
            P(dp, tensor),
            P(dp + tensor, None),
            P(dp, tensor),
            P(dp, None),
            P(dp),
        ),
        out_specs=P(dp, tensor),
        check_vma=False,
    )
```

profile of v0, /device:TPU:1, one launch (start us, length us, event | category | flops | bytes accessed | tf_op | source)
XLA Modules:
  0.0 256.3 jit_solution(8563015465687034795)
XLA Ops:
  6.5 3.2 %collective-permute-start = (bf16[1856,256]{1,0:T(8,128)(2,1)}, bf16[1856,256]{1,0:T(8,128)(2,1)S(1)}, u32[]{:S(2)}, u32[]{:S(2)}) collective-permute-start(bf16[1856,256]{1,0:T(8,128)(2,1)} %param.11), channel_id=1, source_target_pairs={{1,0},{0,1},{3,2},{2,3},{5,4},{4,5},{7,6},{6,7},{9,8},{8,9},{11,10... | collective-permute-start | bytes 2850824 | tf_op jit(solution)/shard_map/ppermute | solution.py:28
  14.3 4.9 %all-to-all-start = ((bf16[16,8,1856]{2,0,1:T(8,128)(2,1)}), bf16[16,8,1856]{2,0,1:T(8,128)(2,1)S(1)}, u32[]{:S(2)}, u32[]{:S(2)}) async-start(bf16[16,8,1856]{2,0,1:T(8,128)(2,1)} %copy.44), calls=%async_computation | async-start | bytes 983040 | tf_op jit(solution)/shard_map/all_to_all | solution.py:191
  19.2 10.5 %all-to-all-done = bf16[16,8,1856]{2,0,1:T(8,128)(2,1)S(1)} async-done(((bf16[16,8,1856]{2,0,1:T(8,128)(2,1)}), bf16[16,8,1856]{2,0,1:T(8,128)(2,1)S(1)}, u32[]{:S(2)}, u32[]{:S(2)}) %all-to-all-start) | async-done | bytes 475168 | tf_op jit(solution)/shard_map/all_to_all | solution.py:191
  34.3 5.7 %collective-permute-start.3 = (bf16[11,16,1856]{2,1,0:T(8,128)(2,1)S(1)}, bf16[11,16,1856]{2,1,0:T(8,128)(2,1)S(1)}, u32[]{:S(2)}, u32[]{:S(2)}) collective-permute-start(bf16[11,16,1856]{2,1,0:T(8,128)(2,1)S(1)} %pad_maximum_fusion.6), channel_id=1, source_target_pairs={{4,0},{8,4},{12,8},{16,12},{20,16},{24,20},{28,24},{0,28},{5,1},{9... | collective-permute-start | bytes 1959944 | tf_op jit(solution)/shard_map/ppermute | solution.py:28
  41.0 5.2 %collective-permute-start.6 = (bf16[8,2,16,256]{3,2,1,0:T(8,128)(2,1)S(1)}, bf16[8,2,16,256]{3,2,1,0:T(8,128)(2,1)S(1)}, u32[]{:S(2)}, u32[]{:S(2)}) collective-permute-start(bf16[8,2,16,256]{3,2,1,0:T(8,128)(2,1)S(1)} %get-tuple-element.93), channel_id=1, source_target_pairs={{1,0},{0,1},{3,2},{2,3},{5,4},{4,5},{7,6},{6,7},{9,8},{8,9},{11,10... | collective-permute-start | bytes 393224 | tf_op jit(solution)/shard_map/ppermute | solution.py:28
  46.9 4.9 %all-to-all-start.1 = ((bf16[32,16,128]{2,1,0:T(8,128)(2,1)}), bf16[32,16,128]{2,1,0:T(8,128)(2,1)S(1)}, u32[]{:S(2)}, u32[]{:S(2)}) async-start(bf16[32,16,128]{2,1,0:T(8,128)(2,1)} %bitcast.7), calls=%async_computation.1 | async-start | bytes 262144 | tf_op jit(solution)/shard_map/all_to_all | solution.py:208
  51.9 3.6 %pad_maximum_fusion.1 = bf16[1856,1024]{1,0:T(8,128)(2,1)} fusion(bf16[1856,256]{1,0:T(8,128)(2,1)} %copy-done.16, bf16[1856,256]{1,0:T(8,128)(2,1)} %param.12, bf16[1856,256]{1,0:T(8,128)(2,1)} %copy-done.15, bf16[1856,256]{1,0:T(8,128)(2,1)} %param.11), kind=kLoop, calls=%fused_computation.1 | loop fusion | flops 15204352 | bytes 7602176 | tf_op jit(solution)/shard_map/concatenate | solution.py:205
  57.3 3.9 %all-to-all-done.1 = bf16[32,16,128]{2,1,0:T(8,128)(2,1)S(1)} async-done(((bf16[32,16,128]{2,1,0:T(8,128)(2,1)}), bf16[32,16,128]{2,1,0:T(8,128)(2,1)S(1)}, u32[]{:S(2)}, u32[]{:S(2)}) %all-to-all-start.1) | async-done | bytes 131104 | tf_op jit(solution)/shard_map/all_to_all | solution.py:208
  66.8 12.8 %collective-permute-done.9 = bf16[2,5,16,1856]{3,2,1,0:T(8,128)(2,1)S(1)} collective-permute-done((bf16[2,5,16,1856]{3,2,1,0:T(8,128)(2,1)S(1)}, bf16[2,5,16,1856]{3,2,1,0:T(8,128)(2,1)S(1)}, u32[]{:S(2)}, u32[]{:S(2)}) %collective-permute-start.9) | collective-permute-done | bytes 593952 | tf_op jit(solution)/shard_map/ppermute | solution.py:28
  89.4 4.5 %convolution_convert_fusion.2 = bf16[768,1024]{1,0:T(8,128)(2,1)} fusion(bf16[768,1856]{1,0:T(8,128)(2,1)S(1)} %bitcast.136, bf16[1856,1024]{1,0:T(8,128)(2,1)S(1)} %copy-done.8), kind=kOutput, calls=%fused_computation.9 | convolution fusion | flops 2920022016 | bytes 8224768 | tf_op jit(solution)/shard_map/dot_general | solution.py:41
  111.5 7.2 %collective-permute-done.17 = bf16[2,64,1024]{2,1,0:T(8,128)(2,1)S(1)} collective-permute-done((bf16[2,64,1024]{2,1,0:T(8,128)(2,1)S(1)}, bf16[2,64,1024]{2,1,0:T(8,128)(2,1)S(1)}, u32[]{:S(2)}, u32[]{:S(2)}) %collective-permute-start.17) | collective-permute-done | bytes 262176 | tf_op jit(solution)/shard_map/ppermute | solution.py:28
  121.1 4.5 %collective-permute-done.18 = bf16[2,64,1024]{2,1,0:T(8,128)(2,1)S(1)} collective-permute-done((bf16[2,64,1024]{2,1,0:T(8,128)(2,1)S(1)}, bf16[2,64,1024]{2,1,0:T(8,128)(2,1)S(1)}, u32[]{:S(2)}, u32[]{:S(2)}) %collective-permute-start.18) | collective-permute-done | bytes 262176 | tf_op jit(solution)/shard_map/ppermute | solution.py:28
  130.8 3.6 %reduce-scatter.2.cloned.1.call-done = bf16[1,192,1024]{2,1,0:T(8,128)(2,1)} async-done(((bf16[4,192,1024]{2,1,0:T(8,128)(2,1)}), bf16[1,192,1024]{2,1,0:T(8,128)(2,1)}) %reduce-scatter.2.cloned.1.call-update) | async-done | bytes 393232 | tf_op jit(solution)/shard_map/reduce_scatter | solution.py:247
  141.0 4.5 %convolution_convert_fusion.1 = bf16[768,1024]{1,0:T(8,128)(2,1)} fusion(bf16[768,1856]{1,0:T(8,128)(2,1)S(1)} %bitcast.138, bf16[1856,1024]{1,0:T(8,128)(2,1)S(1)} %copy-done.10), kind=kOutput, calls=%fused_computation.8 | convolution fusion | flops 2920022016 | bytes 8224768 | tf_op jit(solution)/shard_map/dot_general | solution.py:41
  145.5 3.9 %all-to-all-start.2 = ((bf16[8,96,1024]{2,1,0:T(8,128)(2,1)}), bf16[8,96,1024]{2,1,0:T(8,128)(2,1)S(1)}, u32[]{:S(2)}, u32[]{:S(2)}) async-start(bf16[8,96,1024]{2,1,0:T(8,128)(2,1)} %bitcast.148), calls=%async_computation.3 | async-start | bytes 3145728 | tf_op jit(solution)/shard_map/all_to_all | solution.py:264
  152.6 14.6 %collective-permute-done.21 = bf16[64,1024]{1,0:T(8,128)(2,1)S(1)} collective-permute-done((bf16[64,1024]{1,0:T(8,128)(2,1)S(1)}, bf16[64,1024]{1,0:T(8,128)(2,1)S(1)}, u32[]{:S(2)}, u32[]{:S(2)}) %collective-permute-start.21) | collective-permute-done | bytes 131104 | tf_op jit(solution)/shard_map/ppermute | solution.py:28
  167.2 4.2 %collective-permute-done.20 = bf16[96,1024]{1,0:T(8,128)(2,1)S(1)} collective-permute-done((bf16[96,1024]{1,0:T(8,128)(2,1)}, bf16[96,1024]{1,0:T(8,128)(2,1)S(1)}, u32[]{:S(2)}, u32[]{:S(2)}) %collective-permute-start.20) | collective-permute-done | bytes 196640 | tf_op jit(solution)/shard_map/ppermute | solution.py:28
  171.8 3.7 %shard_map.91 = (f32[256,512]{1,0:T(8,128)S(1)}, f32[256,512]{1,0:T(8,128)S(1)}, f32[1,128]{1,0:T(1,128)S(1)}) custom-call(s32[14]{0:T(128)S(1)} %pad_add_fusion.info_ref, f32[256,1024]{1,0:T(8,128)S(1)} %pad_maximum_fusion.5.both_ref, f32[8,2,16,512]{3,2,1,0:T(8,128)S(1)} %maximum_convert_fusion.read_ref, f32[4,128,128]{2,1,0:T(8,128)S(1)} %bitcast_convert_fusion.1.kv_ref), custom_call_target="tpu_custom_call" | custom-call | tf_op jit(solution)/shard_map/pallas_call | solution.py:133
  177.1 20.3 %all_to_all.36 = f32[32,1,128]{2,1,0:T(1,128)} all-to-all(f32[32,1,128]{2,1,0:T(1,128)S(1)} %broadcast_in_dim.10), channel_id=1, replica_groups=mesh['y'=4,'x_hi'=2,'z'=8,'x_lo'=2,'core'=2] {'z','x_lo','core'}, dimensions={0} | all-to-all | bytes 32768 | tf_op jit(solution)/shard_map/all_to_all | solution.py:271
  202.2 4.7 %all-to-all-start.4 = ((bf16[8,256,512]{2,1,0:T(8,128)(2,1)}), bf16[8,256,512]{2,1,0:T(8,128)(2,1)}, u32[]{:S(2)}, u32[]{:S(2)}) async-start(bf16[8,256,512]{2,1,0:T(8,128)(2,1)} %broadcast_in_dim.11), calls=%async_computation.5 | async-start | bytes 4194304 | tf_op jit(solution)/shard_map/all_to_all | solution.py:275
  206.9 6.0 %pad_maximum_fusion = bf16[8,256,1856]{2,1,0:T(8,128)(2,1)} fusion(bf16[8,96,1856]{2,1,0:T(8,128)(2,1)} %bitcast.139, bf16[8,64,1856]{2,1,0:T(8,128)(2,1)} %bitcast.143, bf16[8,96,1856]{2,1,0:T(8,128)(2,1)S(1)} %bitcast.137), kind=kLoop, calls=%fused_computation | loop fusion | flops 22806528 | bytes 15204352 | tf_op jit(solution)/shard_map/concatenate | solution.py:267
  213.0 21.5 %all-to-all-done.4 = bf16[8,256,512]{2,1,0:T(8,128)(2,1)} async-done(((bf16[8,256,512]{2,1,0:T(8,128)(2,1)}), bf16[8,256,512]{2,1,0:T(8,128)(2,1)}, u32[]{:S(2)}, u32[]{:S(2)}) %all-to-all-start.4) | async-done | bytes 2097184 | tf_op jit(solution)/shard_map/all_to_all | solution.py:275
  234.5 5.8 %convolution_convert_fusion = bf16[1856,256]{1,0:T(8,128)(2,1)S(1)} fusion(bf16[2048,1856]{1,0:T(8,128)(2,1)} %bitcast.140, bf16[2048,512]{1,0:T(8,128)(2,1)} %bitcast.67), kind=kOutput, calls=%fused_computation.5 | convolution fusion | flops 1946632192 | bytes 9863168 | tf_op jit(solution)/shard_map/dot_general | solution.py:278
  244.6 4.9 %convert_add_fusion = f32[1856,256]{1,0:T(8,128)} fusion(bf16[1856,256]{1,0:T(8,128)(2,1)S(1)} %collective-permute-done.22, bf16[2048,1856]{1,0:T(8,128)(2,1)S(1)} %bitcast.141, bf16[2048,512]{1,0:T(8,128)(2,1)} %bitcast.67), kind=kOutput, calls=%fused_computation.7 | convolution fusion | flops 1947107328 | bytes 11501568 | tf_op jit(solution)/shard_map/dot_general | solution.py:278
  (171 shorter events, 73.6 us)
Async XLA Ops:
  6.5 23.2 %collective-permute-start = (bf16[1856,256]{1,0:T(8,128)(2,1)}, bf16[1856,256]{1,0:T(8,128)(2,1)S(1)}, u32[]{:S(2)}, u32[]{:S(2)}) collective-permute-start(bf16[1856,256]{1,0:T(8,128)(2,1)} %param.11), channel_id=1, source_target_pairs={{1,0},{0,1},{3,2},{2,3},{5,4},{4,5},{7,6},{6,7},{9,8},{8,9},{11,10... | collective-permute-start | bytes 2850824 | tf_op jit(solution)/shard_map/ppermute | solution.py:28
  9.8 19.9 %collective-permute-start.1 = (bf16[1856,256]{1,0:T(8,128)(2,1)}, bf16[1856,256]{1,0:T(8,128)(2,1)S(1)}, u32[]{:S(2)}, u32[]{:S(2)}) collective-permute-start(bf16[1856,256]{1,0:T(8,128)(2,1)} %param.12), channel_id=1, source_target_pairs={{1,0},{0,1},{3,2},{2,3},{5,4},{4,5},{7,6},{6,7},{9,8},{8,9},{11,10... | collective-permute-start | bytes 2850824 | tf_op jit(solution)/shard_map/ppermute | solution.py:28
  14.3 15.4 %all-to-all-start = ((bf16[16,8,1856]{2,0,1:T(8,128)(2,1)}), bf16[16,8,1856]{2,0,1:T(8,128)(2,1)S(1)}, u32[]{:S(2)}, u32[]{:S(2)}) async-start(bf16[16,8,1856]{2,0,1:T(8,128)(2,1)} %copy.44), calls=%async_computation | async-start | bytes 983040 | tf_op jit(solution)/shard_map/all_to_all | solution.py:191
  31.0 31.8 %collective-permute-start.5 = (bf16[5,16,1856]{2,1,0:T(8,128)(2,1)}, bf16[5,16,1856]{2,1,0:T(8,128)(2,1)}, u32[]{:S(2)}, u32[]{:S(2)}) collective-permute-start(bf16[5,16,1856]{2,1,0:T(8,128)(2,1)} %slice.106), channel_id=1, source_target_pairs={{2,0},{0,2},{3,1},{1,3},{6,4},{4,6},{7,5},{5,7},{10,8},{8,10},{11,... | collective-permute-start | bytes 890888 | tf_op jit(solution)/shard_map/ppermute | solution.py:28
  34.3 28.5 %collective-permute-start.3 = (bf16[11,16,1856]{2,1,0:T(8,128)(2,1)S(1)}, bf16[11,16,1856]{2,1,0:T(8,128)(2,1)S(1)}, u32[]{:S(2)}, u32[]{:S(2)}) collective-permute-start(bf16[11,16,1856]{2,1,0:T(8,128)(2,1)S(1)} %pad_maximum_fusion.6), channel_id=1, source_target_pairs={{4,0},{8,4},{12,8},{16,12},{20,16},{24,20},{28,24},{0,28},{5,1},{9... | collective-permute-start | bytes 1959944 | tf_op jit(solution)/shard_map/ppermute | solution.py:28
  40.0 22.9 %collective-permute-start.4 = (bf16[11,16,1856]{2,1,0:T(8,128)(2,1)S(1)}, bf16[11,16,1856]{2,1,0:T(8,128)(2,1)S(1)}, u32[]{:S(2)}, u32[]{:S(2)}) collective-permute-start(bf16[11,16,1856]{2,1,0:T(8,128)(2,1)S(1)} %pad_maximum_fusion.6), channel_id=1, source_target_pairs={{28,0},{0,4},{4,8},{8,12},{12,16},{16,20},{20,24},{24,28},{29,1},{... | collective-permute-start | bytes 1959944 | tf_op jit(solution)/shard_map/ppermute | solution.py:28
  41.0 14.7 %collective-permute-start.6 = (bf16[8,2,16,256]{3,2,1,0:T(8,128)(2,1)S(1)}, bf16[8,2,16,256]{3,2,1,0:T(8,128)(2,1)S(1)}, u32[]{:S(2)}, u32[]{:S(2)}) collective-permute-start(bf16[8,2,16,256]{3,2,1,0:T(8,128)(2,1)S(1)} %get-tuple-element.93), channel_id=1, source_target_pairs={{1,0},{0,1},{3,2},{2,3},{5,4},{4,5},{7,6},{6,7},{9,8},{8,9},{11,10... | collective-permute-start | bytes 393224 | tf_op jit(solution)/shard_map/ppermute | solution.py:28
  46.9 14.3 %all-to-all-start.1 = ((bf16[32,16,128]{2,1,0:T(8,128)(2,1)}), bf16[32,16,128]{2,1,0:T(8,128)(2,1)S(1)}, u32[]{:S(2)}, u32[]{:S(2)}) async-start(bf16[32,16,128]{2,1,0:T(8,128)(2,1)} %bitcast.7), calls=%async_computation.1 | async-start | bytes 262144 | tf_op jit(solution)/shard_map/all_to_all | solution.py:208
  51.9 82.6 %reduce-scatter.2.cloned.1.call-start = ((), (), s32[]{:S(2)}) async-start(), calls=%async_computation.6 | async-start | bytes 1966080 | tf_op jit(solution)/shard_map/reduce_scatter | solution.py:247
  62.8 16.9 %collective-permute-start.7 = (bf16[11,16,1856]{2,1,0:T(8,128)(2,1)S(1)}, bf16[11,16,1856]{2,1,0:T(8,128)(2,1)}, u32[]{:S(2)}, u32[]{:S(2)}) collective-permute-start(bf16[11,16,1856]{2,1,0:T(8,128)(2,1)S(1)} %collective-permute-done.3), channel_id=1, source_target_pairs={{4,0},{8,4},{12,8},{16,12},{20,16},{24,20},{28,24},{0,28},{5,1},{9... | collective-permute-start | bytes 1959944 | tf_op jit(solution)/shard_map/ppermute | solution.py:28
  63.0 16.8 %collective-permute-start.8 = (bf16[11,16,1856]{2,1,0:T(8,128)(2,1)S(1)}, bf16[11,16,1856]{2,1,0:T(8,128)(2,1)}, u32[]{:S(2)}, u32[]{:S(2)}) collective-permute-start(bf16[11,16,1856]{2,1,0:T(8,128)(2,1)S(1)} %collective-permute-done.4), channel_id=1, source_target_pairs={{28,0},{0,4},{4,8},{8,12},{12,16},{16,20},{20,24},{24,28},{29,1},{... | collective-permute-start | bytes 1959944 | tf_op jit(solution)/shard_map/ppermute | solution.py:28
  64.6 15.0 %collective-permute-start.9 = (bf16[2,5,16,1856]{3,2,1,0:T(8,128)(2,1)S(1)}, bf16[2,5,16,1856]{3,2,1,0:T(8,128)(2,1)S(1)}, u32[]{:S(2)}, u32[]{:S(2)}) collective-permute-start(bf16[2,5,16,1856]{3,2,1,0:T(8,128)(2,1)S(1)} %pad_maximum_fusion.7), channel_id=1, source_target_pairs={{2,0},{0,2},{3,1},{1,3},{6,4},{4,6},{7,5},{5,7},{10,8},{8,10},{11,... | collective-permute-start | bytes 1781768 | tf_op jit(solution)/shard_map/ppermute | solution.py:28
  80.7 18.3 %collective-permute-start.10 = (bf16[11,16,1856]{2,1,0:T(8,128)(2,1)}, bf16[11,16,1856]{2,1,0:T(8,128)(2,1)S(1)}, u32[]{:S(2)}, u32[]{:S(2)}) collective-permute-start(bf16[11,16,1856]{2,1,0:T(8,128)(2,1)} %collective-permute-done.7), channel_id=1, source_target_pairs={{4,0},{8,4},{12,8},{16,12},{20,16},{24,20},{28,24},{0,28},{5,1},{9... | collective-permute-start | bytes 1959944 | tf_op jit(solution)/shard_map/ppermute | solution.py:28
  82.5 16.6 %collective-permute-start.11 = (bf16[11,16,1856]{2,1,0:T(8,128)(2,1)}, bf16[11,16,1856]{2,1,0:T(8,128)(2,1)S(1)}, u32[]{:S(2)}, u32[]{:S(2)}) collective-permute-start(bf16[11,16,1856]{2,1,0:T(8,128)(2,1)} %collective-permute-done.8), channel_id=1, source_target_pairs={{28,0},{0,4},{4,8},{8,12},{12,16},{16,20},{20,24},{24,28},{29,1},{... | collective-permute-start | bytes 1959944 | tf_op jit(solution)/shard_map/ppermute | solution.py:28
  84.3 13.7 %collective-permute-start.12 = (bf16[2,5,16,1856]{3,2,1,0:T(8,128)(2,1)}, bf16[2,5,16,1856]{3,2,1,0:T(8,128)(2,1)}, u32[]{:S(2)}, u32[]{:S(2)}) collective-permute-start(bf16[2,5,16,1856]{3,2,1,0:T(8,128)(2,1)} %pad_maximum_fusion.8), channel_id=1, source_target_pairs={{2,0},{0,2},{3,1},{1,3},{6,4},{4,6},{7,5},{5,7},{10,8},{8,10},{11,... | collective-permute-start | bytes 1781768 | tf_op jit(solution)/shard_map/ppermute | solution.py:28
  105.2 13.6 %collective-permute-start.17 = (bf16[2,64,1024]{2,1,0:T(8,128)(2,1)S(1)}, bf16[2,64,1024]{2,1,0:T(8,128)(2,1)S(1)}, u32[]{:S(2)}, u32[]{:S(2)}) collective-permute-start(bf16[2,64,1024]{2,1,0:T(8,128)(2,1)S(1)} %get-tuple-element.79), channel_id=1, source_target_pairs={{128,0},{192,64},{0,128},{64,192},{129,1},{193,65},{1,129},{65,193... | collective-permute-start | bytes 786440 | tf_op jit(solution)/shard_map/ppermute | solution.py:28
  105.9 19.8 %collective-permute-start.18 = (bf16[2,64,1024]{2,1,0:T(8,128)(2,1)S(1)}, bf16[2,64,1024]{2,1,0:T(8,128)(2,1)S(1)}, u32[]{:S(2)}, u32[]{:S(2)}) collective-permute-start(bf16[2,64,1024]{2,1,0:T(8,128)(2,1)S(1)} %get-tuple-element.81), channel_id=1, source_target_pairs={{192,0},{0,64},{64,128},{128,192},{193,1},{1,65},{65,129},{129,193... | collective-permute-start | bytes 786440 | tf_op jit(solution)/shard_map/ppermute | solution.py:28
  106.5 19.5 %collective-permute-start.19 = (bf16[2,64,1024]{2,1,0:T(8,128)(2,1)S(1)}, bf16[2,64,1024]{2,1,0:T(8,128)(2,1)S(1)}, u32[]{:S(2)}, u32[]{:S(2)}) collective-permute-start(bf16[2,64,1024]{2,1,0:T(8,128)(2,1)S(1)} %get-tuple-element.80), channel_id=1, source_target_pairs={{64,0},{128,64},{192,128},{0,192},{65,1},{129,65},{193,129},{1,193... | collective-permute-start | bytes 786440 | tf_op jit(solution)/shard_map/ppermute | solution.py:28
  108.7 18.3 %collective-permute-start.15 = (bf16[2,5,16,1856]{3,2,1,0:T(8,128)(2,1)S(1)}, bf16[2,5,16,1856]{3,2,1,0:T(8,128)(2,1)S(1)}, u32[]{:S(2)}, u32[]{:S(2)}) collective-permute-start(bf16[2,5,16,1856]{3,2,1,0:T(8,128)(2,1)S(1)} %pad_maximum_fusion.9), channel_id=1, source_target_pairs={{2,0},{0,2},{3,1},{1,3},{6,4},{4,6},{7,5},{5,7},{10,8},{8,10},{11,... | collective-permute-start | bytes 1781768 | tf_op jit(solution)/shard_map/ppermute | solution.py:28
  110.2 16.7 %collective-permute-start.13 = (bf16[5,16,1856]{2,1,0:T(8,128)(2,1)S(1)}, bf16[5,16,1856]{2,1,0:T(8,128)(2,1)S(1)}, u32[]{:S(2)}, u32[]{:S(2)}) collective-permute-start(bf16[5,16,1856]{2,1,0:T(8,128)(2,1)S(1)} %get-tuple-element.83), channel_id=1, source_target_pairs={{4,0},{8,4},{12,8},{16,12},{20,16},{24,20},{28,24},{0,28},{5,1},{9... | collective-permute-start | bytes 890888 | tf_op jit(solution)/shard_map/ppermute | solution.py:28
  145.5 25.9 %all-to-all-start.2 = ((bf16[8,96,1024]{2,1,0:T(8,128)(2,1)}), bf16[8,96,1024]{2,1,0:T(8,128)(2,1)S(1)}, u32[]{:S(2)}, u32[]{:S(2)}) async-start(bf16[8,96,1024]{2,1,0:T(8,128)(2,1)} %bitcast.148), calls=%async_computation.3 | async-start | bytes 3145728 | tf_op jit(solution)/shard_map/all_to_all | solution.py:264
  149.5 17.7 %collective-permute-start.21 = (bf16[64,1024]{1,0:T(8,128)(2,1)S(1)}, bf16[64,1024]{1,0:T(8,128)(2,1)S(1)}, u32[]{:S(2)}, u32[]{:S(2)}) collective-permute-start(bf16[64,1024]{1,0:T(8,128)(2,1)S(1)} %fusion.10), channel_id=1, source_target_pairs={{32,0},{0,32},{33,1},{1,33},{34,2},{2,34},{35,3},{3,35},{36,4},{4,... | collective-permute-start | bytes 393224 | tf_op jit(solution)/shard_map/ppermute | solution.py:28
  152.4 19.0 %collective-permute-start.20 = (bf16[96,1024]{1,0:T(8,128)(2,1)}, bf16[96,1024]{1,0:T(8,128)(2,1)S(1)}, u32[]{:S(2)}, u32[]{:S(2)}) collective-permute-start(bf16[96,1024]{1,0:T(8,128)(2,1)} %get-tuple-element.90), channel_id=1, source_target_pairs={{32,0},{0,32},{33,1},{1,33},{34,2},{2,34},{35,3},{3,35},{36,4},{4,... | collective-permute-start | bytes 589832 | tf_op jit(solution)/shard_map/ppermute | solution.py:28
  202.2 32.2 %all-to-all-start.4 = ((bf16[8,256,512]{2,1,0:T(8,128)(2,1)}), bf16[8,256,512]{2,1,0:T(8,128)(2,1)}, u32[]{:S(2)}, u32[]{:S(2)}) async-start(bf16[8,256,512]{2,1,0:T(8,128)(2,1)} %broadcast_in_dim.11), calls=%async_computation.5 | async-start | bytes 4194304 | tf_op jit(solution)/shard_map/all_to_all | solution.py:275
  (30 other events, 347.7 us)
Sparse Core Ops, SparseCore 0:
  98.1 36.3 reduce-scatter.1
where the time goes:
time: 258 us; the launch traced here: 256 us
  waiting for transfers between devices  87.6 us (34%)
  starting transfers between devices  56.1 us (22%)
  local copies, waits for them, and re-layouts  25.7 us (10%)
  other arithmetic  24.6 us (10%)
  matrix products  22 us (9%)
  blocking collectives  20.3 us (8%)
  between operations  14.1 us (5%)
  Pallas kernels  5.91 us (2%)
    ppermute x23, waiting for transfers between devices, toward(): return lambda value: lax.ppermute(value, axis, pairs)  48.1 us
    ppermute x23, starting transfers between devices, toward(): return lambda value: lax.ppermute(value, axis, pairs)  37.6 us
    all_to_all x1, waiting for transfers between devices, shards(): lax.all_to_all(hess_all, ('y', 'x_hi'), split_axis=0, concat_axis=0, tile...  21.5 us
    all_to_all x1, blocking collectives, shards(): lax.all_to_all(spread, tensor, split_axis=0, concat_axis=0, tiled=True)  20.3 us
    unnamed x48, local copies, waits for them, and re-layouts  11.6 us
    dot_general x3, matrix products, dot(): return jnp.dot(a, b, preferred_element_type=f32)  11.3 us
    dot_general x2, matrix products, shards(): lax.dot_general(left, b, (((0,), (0,)), ((), ())), preferred_element_type...  10.7 us
    all_to_all x1, waiting for transfers between devices, shards(): lax.all_to_all(normed, ('y', 'x_hi'), split_axis=1, concat_axis=0, tiled=...  10.5 us
  transfers between devices with their start and end apart: 28, of which 13 were waited for; matrix products, arithmetic and copies ran while one was open for 15% of the time, Pallas kernels for 0%

commit v1 on v0

--- a/solution.py
+++ b/solution.py
@@ -12,7 +12,6 @@
 KVH = 8
 NY, NX, NZ, NL, NC = 4, 2, 8, 2, 2
 DP = NY * NX
-EARLY = 3
 
 pair_beta = 0.5
 norm_epsilon = 1e-05
@@ -29,7 +28,6 @@
 
 
 core_swap = toward("core", NC, 1)
-lo_swap = toward("x_lo", NL, 1)
 hi_swap = toward("x_hi", NX, 1)
 
 
@@ -42,18 +40,16 @@
 
 
 def reduce_y(partial, iy):
-    split = partial.reshape(NY, NX, *partial.shape[1:])
-    block = lambda dy: lax.dynamic_index_in_dim(split, lax.rem(iy + dy, NY), 0, False)
-    total = block(0).astype(f32)
-    for part in [toward("y", NY, -dy)(block(dy)) for dy in (2, 1, 3)]:
+    split = partial.reshape(partial.shape[0], NY, NX, *partial.shape[2:])
+    block = lambda dy: lax.dynamic_index_in_dim(split, lax.rem(iy + dy, NY), 1, False)
+    return [block(0)] + [toward("y", NY, -dy)(block(dy)) for dy in (2, 1, 3)]
+
+
+def add(parts):
+    total = parts[0].astype(f32)
+    for part in parts[1:]:
         total = total + part.astype(f32)
     return total
-
-
-def hi_halves(total, ix):
-    keep = lax.dynamic_index_in_dim(total, ix, 0, False)
-    give = lax.dynamic_index_in_dim(total, 1 - ix, 0, False)
-    return keep.astype(f32), hi_swap(give.astype(bf16))
 
 
 def attention_kernel(info_ref, both_ref, read_ref, kv_ref, grad_ref, tan_ref, sums_ref, keys_ref, values_ref):
@@ -74,7 +70,7 @@
     lane = lax.broadcasted_iota(jnp.int32, (part_rows, LANES), 1)
     row = lax.broadcasted_iota(jnp.int32, (part_rows, LANES), 0)
     out_lane = lax.broadcasted_iota(jnp.int32, (1, LANES), 1)
-    x_lo, core = info_ref[chunks + seqs], info_ref[chunks + seqs + 1]
+    core = info_ref[chunks + seqs]
     stack = lambda blocks: jnp.concatenate(blocks, axis=0)
     column = lambda pair: slice(pair * LANES, (pair + 1) * LANES)
     sums = jnp.zeros((1, LANES), f32)
@@ -85,7 +81,7 @@
         length = info_ref[chunks + seq]
         keys, values = keys_ref[seq], values_ref[seq]
         allowed, read = [], []
-        for side in (x_lo, 1 - x_lo):
+        for side in range(sides):
             position = ((place % per_seq * sides + side) * NC + core) * part_rows + row
             allowed.append(lane <= jnp.minimum(position, length - 1))
             live = position[:, :1] < length
@@ -140,7 +136,7 @@
         in_specs=[pl.BlockSpec(memory_space=pltpu.SMEM)] + [vmem] * 3,
         out_specs=(vmem, vmem, vmem),
         scratch_shapes=[pltpu.VMEM((kv.shape[0], 2 * kv.shape[1], LANES), bf16)] * 2,
-        compiler_params=pltpu.CompilerParams(vmem_limit_bytes=24 * 1024 * 1024),
+        compiler_params=pltpu.CompilerParams(vmem_limit_bytes=12 * 1024 * 1024),
     )(info, both, read, kv)
 
 
@@ -175,11 +171,12 @@
         out_shape=jax.ShapeDtypeStruct(grad.shape, f32),
         in_specs=[smem, smem, vmem, vmem, vmem],
         out_specs=vmem,
+        compiler_params=pltpu.CompilerParams(vmem_limit_bytes=6 * 1024 * 1024),
     )(info, ref_margin, spread, grad, tan)
 
 
 def shards(hidden_in, norm_gain, query_weight, probe, key_values, readout, lengths, ref_margin):
-    iy, ix, iz, il, ic = (lax.axis_index(a) for a in ("y", "x_hi", "z", "x_lo", "core"))
+    iy, ix, iz, ic = (lax.axis_index(a) for a in ("y", "x_hi", "z", "core"))
     tensor = ("z", "x_lo", "core")
     rows_here, width = hidden_in.shape
     feats, columns = query_weight.shape
@@ -188,83 +185,59 @@
     stats = jnp.mean(wide * wide, axis=1, keepdims=True)
     normed = (wide * lax.rsqrt(stats + norm_epsilon) * norm_gain.astype(f32)).astype(bf16)
 
-    own = lax.all_to_all(normed, ("y", "x_hi"), split_axis=1, concat_axis=0, tiled=True)
-    own = own.reshape(DP, rows_here, feats)
     other_q, other_t = core_swap(query_weight), core_swap(probe)
-    own, other_q, other_t = together(own, other_q, other_t)
-    message = {0: jnp.concatenate([own, lo_swap(own[:EARLY])])}
-    (message[0],) = together(message[0])
+    sides = normed.reshape(rows_here, DP, feats).swapaxes(0, 1)
+    sides = jnp.broadcast_to(sides[:, None], (DP, NL, rows_here, feats))
+    first = lax.all_to_all(
+        sides.reshape(DP * NL, rows_here, feats), ("y", "x_hi", "x_lo"), split_axis=0, concat_axis=0, tiled=True
+    )
+    chunk = {}
+    chunk[0], other_q, other_t = together(first, other_q, other_t)
 
     seqs = lengths.shape[0] * 2
     seq_len = NZ // seqs * NL * NC * rows_here
-
-    def prepare(token):
-        heads_kv, read, first, second, third, fourth, length, _ = together(
-            key_values, readout, query_weight, other_q, probe, other_t, lengths, token
-        )
-        weights = jnp.concatenate([first, second, third, fourth], axis=1)
-        heads_kv = heads_kv.reshape(rows_here, KVH, 2 * HD).swapaxes(0, 1)
-        heads_kv = jnp.broadcast_to(heads_kv[:, None], (KVH, NL * NC, rows_here, 2 * HD))
-        kv = lax.all_to_all(
-            heads_kv.reshape(NZ * NL * NC, rows_here, 2 * HD), tensor, split_axis=0, concat_axis=0, tiled=True
-        )
-        kv = kv.reshape(seqs, seq_len, 2 * HD).astype(f32)
-        read = read.reshape(NZ, NL, NC, rows_here, columns)
-        mine = lax.dynamic_index_in_dim(read, ic, 2, False)
-        theirs = lax.dynamic_index_in_dim(read, 1 - ic, 2, False)
-        read = jnp.concatenate([mine, core_swap(theirs)], axis=-1).astype(f32)
-        info = jnp.concatenate(
-            [(iz + jnp.array(CHUNKS, jnp.int32) + NZ) % NZ, length.reshape(seqs), jnp.stack([il, ic])]
-        )
-        return weights, info, read, kv
-
     up, down = toward("z", NZ, -1), toward("z", NZ, 1)
 
-    def rows_of(k):
-        return jnp.stack([message[k][:DP], jnp.concatenate([message[k][DP:], late[k]])], axis=1)
-
     def multiply(group):
-        block = jnp.stack([rows_of(k) for k in group], axis=1).reshape(DP, -1, feats)
-        part = dot(block.reshape(-1, feats), weights).astype(bf16)
-        return block, part.reshape(DP, block.shape[1], 4 * columns)
-
-    def swap_late(k):
-        both = lo_swap(jnp.stack([message[k][EARLY:DP], message[-k][EARLY:DP]]))
-        return both[0], both[1]
-
-    late = {}
-    message[1], message[-1] = down(message[0]), up(message[0])
-    late[0] = lo_swap(own[EARLY:])
-    prepared = prepare(message[0])
-    message[1], message[-1], late[0], *prepared = together(message[1], message[-1], late[0], *prepared)
-    weights, info, read, kv = prepared
-    message[2], message[-2] = down(message[1]), up(message[-1])
-    late[1], late[-1] = swap_late(1)
-    message[2], message[-2], late[1], late[-1] = together(message[2], message[-2], late[1], late[-1])
-    message[3], message[-3] = down(message[2]), up(message[-2])
-    late[2], late[-2] = swap_late(2)
-    block_a, part_a = multiply((0, 1, -1))
-    total_a = lax.psum_scatter(part_a.reshape(NY, -1, 4 * columns), "y", scatter_dimension=0, tiled=True)
-    message[3], message[-3], late[2], late[-2], block_a = together(
-        message[3], message[-3], late[2], late[-2], block_a
-    )
-    half = message[0].shape[0] // 2
-    ends = down(message[3][:half]), up(message[-3][half:])
-    late[3], late[-3] = swap_late(3)
-    block_b, part_b = multiply((2, -2))
-    total_b = reduce_y(part_b, iy)
-    *ends, late[3], late[-3], block_b = together(*ends, late[3], late[-3], block_b)
-    message[4] = jnp.concatenate(ends)
-    late[4] = lo_swap(message[4][EARLY:DP])
-    total_a = total_a.reshape(NX, -1, 4 * columns)
-    keep_a, cross_a = hi_halves(total_a, ix)
-    late[4], keep_a, total_b = together(late[4], keep_a, total_b)
-    block_c, part_c = multiply((3, -3, 4))
-    keep_b, cross_b = hi_halves(total_b, ix)
-    arrived = lax.all_to_all(part_c, ("y", "x_hi"), split_axis=0, concat_axis=0, tiled=True)
-    total_c = jnp.sum(arrived.astype(f32), axis=0)
-    projected = jnp.concatenate([keep_a + cross_a.astype(f32), keep_b + cross_b.astype(f32), total_c])
-    normed_all = jnp.concatenate([block_a, block_b, block_c], axis=1)
+        rows = jnp.concatenate([chunk[k] for k in group]).reshape(-1, feats)
+        return dot(rows, weights).astype(bf16).reshape(len(group), DP, NL * rows_here, 4 * columns)
+
+    chunk[1], chunk[-1] = down(chunk[0]), up(chunk[0])
+    heads_kv, _ = together(key_values, chunk[0])
+    heads_kv = heads_kv.reshape(rows_here, KVH, 2 * HD).swapaxes(0, 1)
+    heads_kv = jnp.broadcast_to(heads_kv[:, None], (KVH, NL * NC, rows_here, 2 * HD))
+    kv = lax.all_to_all(
+        heads_kv.reshape(NZ * NL * NC, rows_here, 2 * HD), tensor, split_axis=0, concat_axis=0, tiled=True
+    )
+    weights = jnp.concatenate([query_weight, other_q, probe, other_t], axis=1)
+    chunk[1], chunk[-1], kv, weights = together(chunk[1], chunk[-1], kv, weights)
+    chunk[2], chunk[-2] = down(chunk[1]), up(chunk[-1])
+    moved_a = reduce_y(multiply((0, 1, -1)), iy)
+    chunk[2], chunk[-2], *moved_a = together(chunk[2], chunk[-2], *moved_a)
+    chunk[3], chunk[-3] = down(chunk[2]), up(chunk[-2])
+    moved_b = reduce_y(multiply((2, -2)), iy)
+    total_a = add(moved_a)
+    kv = kv.reshape(seqs, seq_len, 2 * HD).astype(f32)
+    chunk[3], chunk[-3], total_a, kv, *moved_b = together(chunk[3], chunk[-3], total_a, kv, *moved_b)
+    half = DP * NL // 2
+    ends = down(chunk[3][:half]), up(chunk[-3][half:])
+    moved_c = reduce_y(multiply((3, -3)), iy)
+    total_b = add(moved_b)
+    *ends, total_a, total_b = together(*ends, total_a, total_b)
+    chunk[4] = jnp.concatenate(ends)
+    read = readout.reshape(NZ, NL, NC, rows_here, columns)
+    mine = lax.dynamic_index_in_dim(read, ic, 2, False)
+    theirs = lax.dynamic_index_in_dim(read, 1 - ic, 2, False)
+    read = jnp.concatenate([mine, core_swap(theirs)], axis=-1).astype(f32)
+    info = jnp.concatenate([(iz + jnp.array(CHUNKS, jnp.int32) + NZ) % NZ, lengths.reshape(seqs), ic[None]])
+    part_d = multiply((4,))[0]
+    total = jnp.concatenate([total_a, total_b, add(moved_c)])
+    keep = lax.dynamic_index_in_dim(total, ix, 1, False)
+    cross = hi_swap(lax.dynamic_index_in_dim(total, 1 - ix, 1, False).astype(bf16))
+    arrived = lax.all_to_all(part_d, ("y", "x_hi"), split_axis=0, concat_axis=0, tiled=True)
+    last = jnp.sum(arrived.astype(f32), axis=0)
+    projected = jnp.concatenate([(keep + cross.astype(f32)).reshape(-1, 4 * columns), last])
+    normed_all = jnp.stack([chunk[k].reshape(DP, -1, feats) for k in CHUNKS], axis=1)
 
     grad, tan, sums = attention(info, projected, read, kv)
     spread = jnp.broadcast_to(sums[None], (NZ * NL * NC, 1, LANES))

time: 258 us -> 231 us (0.90)
  blocking collectives: 20.3 us -> 38.2 us
  waiting for transfers between devices: 87.6 us -> 73.1 us
  between operations: 14.1 us -> 0.39 us
  other arithmetic: 24.6 us -> 16.6 us
  starting transfers between devices: 56.1 us -> 51.8 us
    all_to_all x0 -> x1, blocking collectives: none -> 20.5 us  [shards(): lax.all_to_all(sides.reshape(DP * NL, rows_here, feats), ('y', 'x_hi', 'x...]
    ppermute x23 -> x22, waiting for transfers between devices: 48.1 us -> 38.1 us  [toward(): return lambda value: lax.ppermute(value, axis, pairs)]
    another operation x22 -> x0, other arithmetic: 5.38 us -> none  [the longest x8 2.42 us: rows_of(): jnp.stack([message[k][:DP], jnp.concatenate([message[k][DP:], late[k]])],...]
    dynamic_slice x0 -> x14, local copies, waits for them, and re-layouts: none -> 5.04 us  [reduce_y(): lax.dynamic_index_in_dim(split, lax.rem(iy + dy, NY), 1, False)]
    all_to_all x1, waiting for transfers between devices: 21.5 us -> 16.8 us  [shards(): lax.all_to_all(hess_all, ('y', 'x_hi'), split_axis=0, concat_axis=0, tile...]
    all_to_all x3 -> x2, waiting for transfers between devices: 14.4 us -> 18.1 us  [the longest x1 16.4 us: shards(): lax.all_to_all(heads_kv.reshape(NZ * NL * NC, rows_here, 2 * HD), tensor,...]
    reduce_scatter x1 -> x0, waiting for transfers between devices: 3.59 us -> none  [shards(): lax.psum_scatter(part_a.reshape(NY, -1, 4 * columns), 'y', scatter_dimens...]
    another operation x13 -> x1, local copies, waits for them, and re-layouts: 4.66 us -> 1.08 us  [shards(): jnp.stack([chunk[k].reshape(DP, -1, feats) for k in CHUNKS], axis=1)]
  transfers between devices with their start and end apart: 28 -> 25, of which waited for: 13 -> 13; matrix products, arithmetic and copies ran while one was open for 15% -> 19% of each run, Pallas kernels for 0% -> 0%
where the time goes in v1:
time: 231 us
  waiting for transfers between devices  73.1 us (32%)
  starting transfers between devices  51.8 us (22%)
  blocking collectives  38.2 us (17%)
  local copies, waits for them, and re-layouts  23.4 us (10%)
  matrix products  22.8 us (10%)
  other arithmetic  16.6 us (7%)
  Pallas kernels  4.34 us (2%)
    ppermute x22, waiting for transfers between devices, toward(): return lambda value: lax.ppermute(value, axis, pairs)  38.1 us
    ppermute x22, starting transfers between devices, toward(): return lambda value: lax.ppermute(value, axis, pairs)  34.2 us
    all_to_all x1, blocking collectives, shards(): lax.all_to_all(sides.reshape(DP * NL, rows_here, feats), ('y', 'x_hi', 'x...  20.5 us
    all_to_all x1, blocking collectives, shards(): lax.all_to_all(spread, tensor, split_axis=0, concat_axis=0, tiled=True)  17.7 us
    all_to_all x1, waiting for transfers between devices, shards(): lax.all_to_all(hess_all, ('y', 'x_hi'), split_axis=0, concat_axis=0, tile...  16.8 us
    all_to_all x1, waiting for transfers between devices, shards(): lax.all_to_all(heads_kv.reshape(NZ * NL * NC, rows_here, 2 * HD), tensor,...  16.4 us
    unnamed x43, local copies, waits for them, and re-layouts  12.8 us
    dot_general x2, matrix products, shards(): lax.dot_general(left, b, (((0,), (0,)), ((), ())), preferred_element_type...  12.6 us
  transfers between devices with their start and end apart: 25, of which 13 were waited for; matrix products, arithmetic and copies ran while one was open for 19% of the time, Pallas kernels for 0%

profile of v1, /device:TPU:1, one launch (start us, length us, event | category | flops | bytes accessed | tf_op | source)
XLA Modules:
  0.0 230.6 jit_solution(15011769248177639243)
XLA Ops:
  0.0 3.2 %collective-permute-start = (bf16[1856,256]{1,0:T(8,128)(2,1)}, bf16[1856,256]{1,0:T(8,128)(2,1)S(1)}, u32[]{:S(2)}, u32[]{:S(2)}) collective-permute-start(bf16[1856,256]{1,0:T(8,128)(2,1)} %param.11), channel_id=1, source_target_pairs={{1,0},{0,1},{3,2},{2,3},{5,4},{4,5},{7,6},{6,7},{9,8},{8,9},{11,10... | collective-permute-start | bytes 2850824 | tf_op jit(solution)/shard_map/ppermute | solution.py:27
  7.0 20.5 %all_to_all.25 = bf16[16,16,1856]{2,1,0:T(8,128)(2,1)S(1)} all-to-all(bf16[16,16,1856]{2,1,0:T(8,128)(2,1)S(1)} %bitcast.101), channel_id=1, replica_groups=mesh['y'=4,'x_hi'=2,'z'=8,'x_lo'=2,'core'=2] {'y','x_hi','x_lo'}, dimensions={0} | all-to-all | bytes 1900544 | tf_op jit(solution)/shard_map/all_to_all | solution.py:191
  28.4 5.6 %collective-permute-start.2 = (bf16[16,16,1856]{2,1,0:T(8,128)(2,1)S(1)}, bf16[16,16,1856]{2,1,0:T(8,128)(2,1)S(1)}, u32[]{:S(2)}, u32[]{:S(2)}) collective-permute-start(bf16[16,16,1856]{2,1,0:T(8,128)(2,1)S(1)} %all_to_all.25), channel_id=1, source_target_pairs={{4,0},{8,4},{12,8},{16,12},{20,16},{24,20},{28,24},{0,28},{5,1},{9... | collective-permute-start | bytes 2850824 | tf_op jit(solution)/shard_map/ppermute | solution.py:27
  34.7 6.9 %all-to-all-start.1 = ((bf16[32,16,128]{2,1,0:T(8,128)(2,1)}), bf16[32,16,128]{2,1,0:T(8,128)(2,1)S(1)}, u32[]{:S(2)}, u32[]{:S(2)}) async-start(bf16[32,16,128]{2,1,0:T(8,128)(2,1)} %bitcast.4), calls=%async_computation.1 | async-start | bytes 262144 | tf_op jit(solution)/shard_map/all_to_all | solution.py:209
  41.6 3.6 %pad_maximum_fusion = bf16[1856,1024]{1,0:T(8,128)(2,1)} fusion(bf16[1856,256]{1,0:T(8,128)(2,1)} %collective-permute-done.1, bf16[1856,256]{1,0:T(8,128)(2,1)} %param.12, bf16[1856,256]{1,0:T(8,128)(2,1)} %copy-done.12, bf16[1856,256]{1,0:T(8,128)(2,1)} %param.11), kind=kLoop, calls=%fused_computation | loop fusion | flops 15204352 | bytes 7602176 | tf_op jit(solution)/shard_map/concatenate | solution.py:212
  45.2 16.4 %all-to-all-done.1 = bf16[32,16,128]{2,1,0:T(8,128)(2,1)S(1)} async-done(((bf16[32,16,128]{2,1,0:T(8,128)(2,1)}), bf16[32,16,128]{2,1,0:T(8,128)(2,1)S(1)}, u32[]{:S(2)}, u32[]{:S(2)}) %all-to-all-start.1) | async-done | bytes 131104 | tf_op jit(solution)/shard_map/all_to_all | solution.py:209
  64.4 3.4 %convolution_convert_fusion.1 = bf16[768,1024]{1,0:T(8,128)(2,1)S(1)} fusion(bf16[768,1856]{1,0:T(8,128)(2,1)S(1)} %bitcast.103, bf16[1856,1024]{1,0:T(8,128)(2,1)S(1)} %copy-done.8), kind=kOutput, calls=%fused_computation.7 | convolution fusion | flops 2920022016 | bytes 8224768 | tf_op jit(solution)/shard_map/dot_general | solution.py:39
  76.9 4.7 %collective-permute-done.6 = bf16[3,2,32,1024]{3,2,0,1:T(8,128)(2,1)} collective-permute-done((bf16[3,2,32,1024]{3,2,0,1:T(8,128)(2,1)}, bf16[3,2,32,1024]{3,2,0,1:T(8,128)(2,1)}, u32[]{:S(2)}, u32[]{:S(2)}) %collective-permute-start.6) | collective-permute-done | bytes 393248 | tf_op jit(solution)/shard_map/ppermute | solution.py:27
  81.7 9.1 %collective-permute-done.7 = bf16[3,2,32,1024]{3,2,0,1:T(8,128)(2,1)} collective-permute-done((bf16[3,2,32,1024]{3,2,0,1:T(8,128)(2,1)}, bf16[3,2,32,1024]{3,2,0,1:T(8,128)(2,1)}, u32[]{:S(2)}, u32[]{:S(2)}) %collective-permute-start.7) | collective-permute-done | bytes 393248 | tf_op jit(solution)/shard_map/ppermute | solution.py:27
  94.1 2.3 %convolution_convert_fusion.3 = bf16[512,1024]{1,0:T(8,128)(2,1)S(1)} fusion(bf16[512,1856]{1,0:T(8,128)(2,1)S(1)} %bitcast.107, bf16[1856,1024]{1,0:T(8,128)(2,1)S(1)} %copy-done.9), kind=kOutput, calls=%fused_computation.9 | convolution fusion | flops 1946681344 | bytes 6750208 | tf_op jit(solution)/shard_map/dot_general | solution.py:39
  98.1 2.4 %collective-permute-start.13 = (bf16[2,2,32,1024]{3,2,0,1:T(8,128)(2,1)S(1)}, bf16[2,2,32,1024]{3,2,0,1:T(8,128)(2,1)S(1)}, u32[]{:S(2)}, u32[]{:S(2)}) collective-permute-start(bf16[2,2,32,1024]{3,2,0,1:T(8,128)(2,1)S(1)} %bitcast.122), channel_id=1, source_target_pairs={{64,0},{128,64},{192,128},{0,192},{65,1},{129,65},{193,129},{1,193... | collective-permute-start | bytes 786440 | tf_op jit(solution)/shard_map/ppermute | solution.py:27
  101.9 3.0 %collective-permute-done.11 = bf16[2,2,32,1024]{3,2,0,1:T(8,128)(2,1)S(1)} collective-permute-done((bf16[2,2,32,1024]{3,2,0,1:T(8,128)(2,1)S(1)}, bf16[2,2,32,1024]{3,2,0,1:T(8,128)(2,1)S(1)}, u32[]{:S(2)}, u32[]{:S(2)}) %collective-permute-start.11) | collective-permute-done | bytes 262176 | tf_op jit(solution)/shard_map/ppermute | solution.py:27
  104.9 7.1 %collective-permute-done.12 = bf16[2,2,32,1024]{3,2,0,1:T(8,128)(2,1)S(1)} collective-permute-done((bf16[2,2,32,1024]{3,2,0,1:T(8,128)(2,1)S(1)}, bf16[2,2,32,1024]{3,2,0,1:T(8,128)(2,1)S(1)}, u32[]{:S(2)}, u32[]{:S(2)}) %collective-permute-start.12) | collective-permute-done | bytes 262176 | tf_op jit(solution)/shard_map/ppermute | solution.py:27
  122.5 2.9 %collective-permute-done.18 = bf16[2,2,32,1024]{3,2,0,1:T(8,128)(2,1)S(1)} collective-permute-done((bf16[2,2,32,1024]{3,2,0,1:T(8,128)(2,1)S(1)}, bf16[2,2,32,1024]{3,2,0,1:T(8,128)(2,1)S(1)}, u32[]{:S(2)}, u32[]{:S(2)}) %collective-permute-start.18) | collective-permute-done | bytes 262176 | tf_op jit(solution)/shard_map/ppermute | solution.py:27
  125.3 5.9 %collective-permute-start.20 = (bf16[8,2,16,256]{3,2,1,0:T(8,128)(2,1)}, bf16[8,2,16,256]{3,2,1,0:T(8,128)(2,1)}, u32[]{:S(2)}, u32[]{:S(2)}) collective-permute-start(bf16[8,2,16,256]{3,2,1,0:T(8,128)(2,1)} %get-tuple-element.76), channel_id=1, source_target_pairs={{1,0},{0,1},{3,2},{2,3},{5,4},{4,5},{7,6},{6,7},{9,8},{8,9},{11,10... | collective-permute-start | bytes 393224 | tf_op jit(solution)/shard_map/ppermute | solution.py:27
  134.5 4.5 %all-to-all-start.2 = ((bf16[8,32,1024]{2,1,0:T(8,128)(2,1)}), bf16[8,32,1024]{2,1,0:T(8,128)(2,1)}, u32[]{:S(2)}, u32[]{:S(2)}) async-start(bf16[8,32,1024]{2,1,0:T(8,128)(2,1)} %bitcast.115), calls=%async_computation.2 | async-start | bytes 1048576 | tf_op jit(solution)/shard_map/all_to_all | solution.py:237
  142.3 2.9 %collective-permute-start.19 = (bf16[7,32,1024]{2,1,0:T(8,128)(2,1)}, bf16[7,32,1024]{2,1,0:T(8,128)(2,1)S(1)}, u32[]{:S(2)}, u32[]{:S(2)}) collective-permute-start(bf16[7,32,1024]{2,1,0:T(8,128)(2,1)} %fusion.10), channel_id=1, source_target_pairs={{32,0},{0,32},{33,1},{1,33},{34,2},{2,34},{35,3},{3,35},{36,4},{4,... | collective-permute-start | bytes 1376264 | tf_op jit(solution)/shard_map/ppermute | solution.py:27
  149.3 5.7 %collective-permute-done.19 = bf16[7,32,1024]{2,1,0:T(8,128)(2,1)S(1)} collective-permute-done((bf16[7,32,1024]{2,1,0:T(8,128)(2,1)}, bf16[7,32,1024]{2,1,0:T(8,128)(2,1)S(1)}, u32[]{:S(2)}, u32[]{:S(2)}) %collective-permute-start.19) | collective-permute-done | bytes 458784 | tf_op jit(solution)/shard_map/ppermute | solution.py:27
  156.4 3.6 %shard_map.91 = (f32[256,512]{1,0:T(8,128)S(1)}, f32[256,512]{1,0:T(8,128)S(1)}, f32[1,128]{1,0:T(1,128)S(1)}) custom-call(s32[13]{0:T(128)S(1)} %pad_add_fusion.info_ref, f32[256,1024]{1,0:T(8,128)S(1)} %pad_maximum_fusion.5.both_ref, f32[8,2,16,512]{3,2,1,0:T(8,128)S(1)} %maximum_convert_fusion.read_ref, f32[4,128,128]{2,1,0:T(8,128)S(1)} %bitcast_convert_fusion.kv_ref), custom_call_target="tpu_custom_call" | custom-call | tf_op jit(solution)/shard_map/pallas_call | solution.py:129
  160.1 17.7 %all_to_all.26 = f32[32,1,128]{2,1,0:T(1,128)S(1)} all-to-all(f32[32,1,128]{2,1,0:T(1,128)S(1)} %broadcast_in_dim.16), channel_id=1, replica_groups=mesh['y'=4,'x_hi'=2,'z'=8,'x_lo'=2,'core'=2] {'z','x_lo','core'}, dimensions={0} | all-to-all | bytes 32768 | tf_op jit(solution)/shard_map/all_to_all | solution.py:244
  180.0 6.2 %all-to-all-start.4 = ((bf16[8,256,512]{2,1,0:T(8,128)(2,1)}), bf16[8,256,512]{2,1,0:T(8,128)(2,1)}, u32[]{:S(2)}, u32[]{:S(2)}) async-start(bf16[8,256,512]{2,1,0:T(8,128)(2,1)} %broadcast_in_dim.17), calls=%async_computation.4 | async-start | bytes 4194304 | tf_op jit(solution)/shard_map/all_to_all | solution.py:248
  197.1 16.8 %all-to-all-done.4 = bf16[8,256,512]{2,1,0:T(8,128)(2,1)} async-done(((bf16[8,256,512]{2,1,0:T(8,128)(2,1)}), bf16[8,256,512]{2,1,0:T(8,128)(2,1)}, u32[]{:S(2)}, u32[]{:S(2)}) %all-to-all-start.4) | async-done | bytes 2097184 | tf_op jit(solution)/shard_map/all_to_all | solution.py:248
  213.9 5.7 %convolution_convert_fusion = bf16[1856,256]{1,0:T(8,128)(2,1)S(1)} fusion(bf16[2048,1856]{1,0:T(8,128)(2,1)} %bitcast.25, bf16[2048,512]{1,0:T(8,128)(2,1)} %bitcast.43), kind=kOutput, calls=%fused_computation.2 | convolution fusion | flops 1946632192 | bytes 9863168 | tf_op jit(solution)/shard_map/dot_general | solution.py:251
  223.7 6.9 %convert_add_fusion = f32[1856,256]{1,0:T(8,128)} fusion(bf16[1856,256]{1,0:T(8,128)(2,1)S(1)} %collective-permute-done.21, bf16[2048,1856]{1,0:T(8,128)(2,1)} %bitcast.25, bf16[2048,512]{1,0:T(8,128)(2,1)} %bitcast.43), kind=kOutput, calls=%fused_computation.5 | convolution fusion | flops 1947107328 | bytes 11763712 | tf_op jit(solution)/shard_map/dot_general | solution.py:251
  (127 shorter events, 63.3 us)
Async XLA Ops:
  0.0 27.5 %collective-permute-start = (bf16[1856,256]{1,0:T(8,128)(2,1)}, bf16[1856,256]{1,0:T(8,128)(2,1)S(1)}, u32[]{:S(2)}, u32[]{:S(2)}) collective-permute-start(bf16[1856,256]{1,0:T(8,128)(2,1)} %param.11), channel_id=1, source_target_pairs={{1,0},{0,1},{3,2},{2,3},{5,4},{4,5},{7,6},{6,7},{9,8},{8,9},{11,10... | collective-permute-start | bytes 2850824 | tf_op jit(solution)/shard_map/ppermute | solution.py:27
  3.2 25.2 %collective-permute-start.1 = (bf16[1856,256]{1,0:T(8,128)(2,1)}, bf16[1856,256]{1,0:T(8,128)(2,1)}, u32[]{:S(2)}, u32[]{:S(2)}) collective-permute-start(bf16[1856,256]{1,0:T(8,128)(2,1)} %param.12), channel_id=1, source_target_pairs={{1,0},{0,1},{3,2},{2,3},{5,4},{4,5},{7,6},{6,7},{9,8},{8,9},{11,10... | collective-permute-start | bytes 2850824 | tf_op jit(solution)/shard_map/ppermute | solution.py:27
  28.4 33.2 %collective-permute-start.2 = (bf16[16,16,1856]{2,1,0:T(8,128)(2,1)S(1)}, bf16[16,16,1856]{2,1,0:T(8,128)(2,1)S(1)}, u32[]{:S(2)}, u32[]{:S(2)}) collective-permute-start(bf16[16,16,1856]{2,1,0:T(8,128)(2,1)S(1)} %all_to_all.25), channel_id=1, source_target_pairs={{4,0},{8,4},{12,8},{16,12},{20,16},{24,20},{28,24},{0,28},{5,1},{9... | collective-permute-start | bytes 2850824 | tf_op jit(solution)/shard_map/ppermute | solution.py:27
  34.0 27.6 %collective-permute-start.3 = (bf16[16,16,1856]{2,1,0:T(8,128)(2,1)S(1)}, bf16[16,16,1856]{2,1,0:T(8,128)(2,1)S(1)}, u32[]{:S(2)}, u32[]{:S(2)}) collective-permute-start(bf16[16,16,1856]{2,1,0:T(8,128)(2,1)S(1)} %all_to_all.25), channel_id=1, source_target_pairs={{28,0},{0,4},{4,8},{8,12},{12,16},{16,20},{20,24},{24,28},{29,1},{... | collective-permute-start | bytes 2850824 | tf_op jit(solution)/shard_map/ppermute | solution.py:27
  34.7 26.9 %all-to-all-start.1 = ((bf16[32,16,128]{2,1,0:T(8,128)(2,1)}), bf16[32,16,128]{2,1,0:T(8,128)(2,1)S(1)}, u32[]{:S(2)}, u32[]{:S(2)}) async-start(bf16[32,16,128]{2,1,0:T(8,128)(2,1)} %bitcast.4), calls=%async_computation.1 | async-start | bytes 262144 | tf_op jit(solution)/shard_map/all_to_all | solution.py:209
  61.6 29.2 %collective-permute-start.4 = (bf16[16,16,1856]{2,1,0:T(8,128)(2,1)S(1)}, bf16[16,16,1856]{2,1,0:T(8,128)(2,1)}, u32[]{:S(2)}, u32[]{:S(2)}) collective-permute-start(bf16[16,16,1856]{2,1,0:T(8,128)(2,1)S(1)} %collective-permute-done.2), channel_id=1, source_target_pairs={{4,0},{8,4},{12,8},{16,12},{20,16},{24,20},{28,24},{0,28},{5,1},{9... | collective-permute-start | bytes 2850824 | tf_op jit(solution)/shard_map/ppermute | solution.py:27
  61.9 28.9 %collective-permute-start.5 = (bf16[16,16,1856]{2,1,0:T(8,128)(2,1)S(1)}, bf16[16,16,1856]{2,1,0:T(8,128)(2,1)}, u32[]{:S(2)}, u32[]{:S(2)}) collective-permute-start(bf16[16,16,1856]{2,1,0:T(8,128)(2,1)S(1)} %collective-permute-done.3), channel_id=1, source_target_pairs={{28,0},{0,4},{4,8},{8,12},{12,16},{16,20},{20,24},{24,28},{29,1},{... | collective-permute-start | bytes 2850824 | tf_op jit(solution)/shard_map/ppermute | solution.py:27
  69.5 12.2 %collective-permute-start.6 = (bf16[3,2,32,1024]{3,2,0,1:T(8,128)(2,1)}, bf16[3,2,32,1024]{3,2,0,1:T(8,128)(2,1)}, u32[]{:S(2)}, u32[]{:S(2)}) collective-permute-start(bf16[3,2,32,1024]{3,2,0,1:T(8,128)(2,1)} %bitcast.84), channel_id=1, source_target_pairs={{128,0},{192,64},{0,128},{64,192},{129,1},{193,65},{1,129},{65,193... | collective-permute-start | bytes 1179656 | tf_op jit(solution)/shard_map/ppermute | solution.py:27
  71.2 19.5 %collective-permute-start.7 = (bf16[3,2,32,1024]{3,2,0,1:T(8,128)(2,1)}, bf16[3,2,32,1024]{3,2,0,1:T(8,128)(2,1)}, u32[]{:S(2)}, u32[]{:S(2)}) collective-permute-start(bf16[3,2,32,1024]{3,2,0,1:T(8,128)(2,1)} %bitcast.83), channel_id=1, source_target_pairs={{192,0},{0,64},{64,128},{128,192},{193,1},{1,65},{65,129},{129,193... | collective-permute-start | bytes 1179656 | tf_op jit(solution)/shard_map/ppermute | solution.py:27
  72.5 18.3 %collective-permute-start.8 = (bf16[3,2,32,1024]{3,2,0,1:T(8,128)(2,1)}, bf16[3,2,32,1024]{3,2,0,1:T(8,128)(2,1)}, u32[]{:S(2)}, u32[]{:S(2)}) collective-permute-start(bf16[3,2,32,1024]{3,2,0,1:T(8,128)(2,1)} %bitcast.82), channel_id=1, source_target_pairs={{64,0},{128,64},{192,128},{0,192},{65,1},{129,65},{193,129},{1,193... | collective-permute-start | bytes 1179656 | tf_op jit(solution)/shard_map/ppermute | solution.py:27
  90.8 23.1 %collective-permute-start.9 = (bf16[16,16,1856]{2,1,0:T(8,128)(2,1)}, bf16[16,16,1856]{2,1,0:T(8,128)(2,1)S(1)}, u32[]{:S(2)}, u32[]{:S(2)}) collective-permute-start(bf16[16,16,1856]{2,1,0:T(8,128)(2,1)} %collective-permute-done.4), channel_id=1, source_target_pairs={{4,0},{8,4},{12,8},{16,12},{20,16},{24,20},{28,24},{0,28},{5,1},{9... | collective-permute-start | bytes 2850824 | tf_op jit(solution)/shard_map/ppermute | solution.py:27
  91.4 23.9 %collective-permute-start.10 = (bf16[16,16,1856]{2,1,0:T(8,128)(2,1)}, bf16[16,16,1856]{2,1,0:T(8,128)(2,1)S(1)}, u32[]{:S(2)}, u32[]{:S(2)}) collective-permute-start(bf16[16,16,1856]{2,1,0:T(8,128)(2,1)} %collective-permute-done.5), channel_id=1, source_target_pairs={{28,0},{0,4},{4,8},{8,12},{12,16},{16,20},{20,24},{24,28},{29,1},{... | collective-permute-start | bytes 2850824 | tf_op jit(solution)/shard_map/ppermute | solution.py:27
  96.5 8.4 %collective-permute-start.11 = (bf16[2,2,32,1024]{3,2,0,1:T(8,128)(2,1)S(1)}, bf16[2,2,32,1024]{3,2,0,1:T(8,128)(2,1)S(1)}, u32[]{:S(2)}, u32[]{:S(2)}) collective-permute-start(bf16[2,2,32,1024]{3,2,0,1:T(8,128)(2,1)S(1)} %bitcast.118), channel_id=1, source_target_pairs={{128,0},{192,64},{0,128},{64,192},{129,1},{193,65},{1,129},{65,193... | collective-permute-start | bytes 786440 | tf_op jit(solution)/shard_map/ppermute | solution.py:27
  97.6 14.4 %collective-permute-start.12 = (bf16[2,2,32,1024]{3,2,0,1:T(8,128)(2,1)S(1)}, bf16[2,2,32,1024]{3,2,0,1:T(8,128)(2,1)S(1)}, u32[]{:S(2)}, u32[]{:S(2)}) collective-permute-start(bf16[2,2,32,1024]{3,2,0,1:T(8,128)(2,1)S(1)} %bitcast.121), channel_id=1, source_target_pairs={{192,0},{0,64},{64,128},{128,192},{193,1},{1,65},{65,129},{129,193... | collective-permute-start | bytes 786440 | tf_op jit(solution)/shard_map/ppermute | solution.py:27
  98.1 13.9 %collective-permute-start.13 = (bf16[2,2,32,1024]{3,2,0,1:T(8,128)(2,1)S(1)}, bf16[2,2,32,1024]{3,2,0,1:T(8,128)(2,1)S(1)}, u32[]{:S(2)}, u32[]{:S(2)}) collective-permute-start(bf16[2,2,32,1024]{3,2,0,1:T(8,128)(2,1)S(1)} %bitcast.122), channel_id=1, source_target_pairs={{64,0},{128,64},{192,128},{0,192},{65,1},{129,65},{193,129},{1,193... | collective-permute-start | bytes 786440 | tf_op jit(solution)/shard_map/ppermute | solution.py:27
  115.7 16.7 %collective-permute-start.14 = (bf16[8,16,1856]{2,1,0:T(8,128)(2,1)S(1)}, bf16[8,16,1856]{2,1,0:T(8,128)(2,1)S(1)}, u32[]{:S(2)}, u32[]{:S(2)}) collective-permute-start(bf16[8,16,1856]{2,1,0:T(8,128)(2,1)S(1)} %slice.12), channel_id=1, source_target_pairs={{4,0},{8,4},{12,8},{16,12},{20,16},{24,20},{28,24},{0,28},{5,1},{9... | collective-permute-start | bytes 1425416 | tf_op jit(solution)/shard_map/ppermute | solution.py:27
  116.1 16.3 %collective-permute-start.15 = (bf16[8,16,1856]{2,1,0:T(8,128)(2,1)S(1)}, bf16[8,16,1856]{2,1,0:T(8,128)(2,1)S(1)}, u32[]{:S(2)}, u32[]{:S(2)}) collective-permute-start(bf16[8,16,1856]{2,1,0:T(8,128)(2,1)S(1)} %slice.13), channel_id=1, source_target_pairs={{28,0},{0,4},{4,8},{8,12},{12,16},{16,20},{20,24},{24,28},{29,1},{... | collective-permute-start | bytes 1425416 | tf_op jit(solution)/shard_map/ppermute | solution.py:27
  119.7 5.7 %collective-permute-start.18 = (bf16[2,2,32,1024]{3,2,0,1:T(8,128)(2,1)S(1)}, bf16[2,2,32,1024]{3,2,0,1:T(8,128)(2,1)S(1)}, u32[]{:S(2)}, u32[]{:S(2)}) collective-permute-start(bf16[2,2,32,1024]{3,2,0,1:T(8,128)(2,1)S(1)} %bitcast.119), channel_id=1, source_target_pairs={{64,0},{128,64},{192,128},{0,192},{65,1},{129,65},{193,129},{1,193... | collective-permute-start | bytes 786440 | tf_op jit(solution)/shard_map/ppermute | solution.py:27
  120.5 10.8 %collective-permute-start.17 = (bf16[2,2,32,1024]{3,2,0,1:T(8,128)(2,1)S(1)}, bf16[2,2,32,1024]{3,2,0,1:T(8,128)(2,1)S(1)}, u32[]{:S(2)}, u32[]{:S(2)}) collective-permute-start(bf16[2,2,32,1024]{3,2,0,1:T(8,128)(2,1)S(1)} %bitcast.117), channel_id=1, source_target_pairs={{192,0},{0,64},{64,128},{128,192},{193,1},{1,65},{65,129},{129,193... | collective-permute-start | bytes 786440 | tf_op jit(solution)/shard_map/ppermute | solution.py:27
  121.4 10.0 %collective-permute-start.16 = (bf16[2,2,32,1024]{3,2,0,1:T(8,128)(2,1)S(1)}, bf16[2,2,32,1024]{3,2,0,1:T(8,128)(2,1)S(1)}, u32[]{:S(2)}, u32[]{:S(2)}) collective-permute-start(bf16[2,2,32,1024]{3,2,0,1:T(8,128)(2,1)S(1)} %bitcast.120), channel_id=1, source_target_pairs={{128,0},{192,64},{0,128},{64,192},{129,1},{193,65},{1,129},{65,193... | collective-permute-start | bytes 786440 | tf_op jit(solution)/shard_map/ppermute | solution.py:27
  125.3 20.0 %collective-permute-start.20 = (bf16[8,2,16,256]{3,2,1,0:T(8,128)(2,1)}, bf16[8,2,16,256]{3,2,1,0:T(8,128)(2,1)}, u32[]{:S(2)}, u32[]{:S(2)}) collective-permute-start(bf16[8,2,16,256]{3,2,1,0:T(8,128)(2,1)} %get-tuple-element.76), channel_id=1, source_target_pairs={{1,0},{0,1},{3,2},{2,3},{5,4},{4,5},{7,6},{6,7},{9,8},{8,9},{11,10... | collective-permute-start | bytes 393224 | tf_op jit(solution)/shard_map/ppermute | solution.py:27
  134.5 13.6 %all-to-all-start.2 = ((bf16[8,32,1024]{2,1,0:T(8,128)(2,1)}), bf16[8,32,1024]{2,1,0:T(8,128)(2,1)}, u32[]{:S(2)}, u32[]{:S(2)}) async-start(bf16[8,32,1024]{2,1,0:T(8,128)(2,1)} %bitcast.115), calls=%async_computation.2 | async-start | bytes 1048576 | tf_op jit(solution)/shard_map/all_to_all | solution.py:237
  142.3 12.7 %collective-permute-start.19 = (bf16[7,32,1024]{2,1,0:T(8,128)(2,1)}, bf16[7,32,1024]{2,1,0:T(8,128)(2,1)S(1)}, u32[]{:S(2)}, u32[]{:S(2)}) collective-permute-start(bf16[7,32,1024]{2,1,0:T(8,128)(2,1)} %fusion.10), channel_id=1, source_target_pairs={{32,0},{0,32},{33,1},{1,33},{34,2},{2,34},{35,3},{3,35},{36,4},{4,... | collective-permute-start | bytes 1376264 | tf_op jit(solution)/shard_map/ppermute | solution.py:27
  180.0 33.9 %all-to-all-start.4 = ((bf16[8,256,512]{2,1,0:T(8,128)(2,1)}), bf16[8,256,512]{2,1,0:T(8,128)(2,1)}, u32[]{:S(2)}, u32[]{:S(2)}) async-start(bf16[8,256,512]{2,1,0:T(8,128)(2,1)} %broadcast_in_dim.17), calls=%async_computation.4 | async-start | bytes 4194304 | tf_op jit(solution)/shard_map/all_to_all | solution.py:248
  (18 other events, 165.8 us)
